TPU v7x, 32 devices: a whole 2x2x4 slice. The times are simulated.
32 devices in a mesh: hb: 4 (over x, core), wb: 2 (over y), hd: 4 (over z).
Axes of the slice: x: 2, y: 2, z: 4, core: 2. Of those that a mesh axis runs over, the one named last changes fastest.
Arguments:
- query_rows: bfloat16 [12, 4, 4, 64, 128], P('hd', 'hb', 'wb'), may hold values from -180 to 180
- key_rows: bfloat16 [12, 4, 4, 64, 128], P('hd', 'hb', 'wb'), may hold values from -6 to 6
- value_rows: bfloat16 [12, 4, 4, 64, 128], P('hd', 'hb', 'wb'), may hold values from -6 to 6
- grad_out: bfloat16 [12, 4, 4, 64, 128], P('hd', 'hb', 'wb'), may hold values from -6 to 6
- sel_tiles: int32 [4, 4, 8], P(None, 'wb'), may hold values from 0 to 7
- sel_count: int32 [4, 4], P(None, 'wb'), may hold values from 1 to 8, as said below
- tile_radius: int32 [12], P('hd'), may hold values from 0 to 1
Outputs:
- grad_query: bfloat16 [12, 4, 4, 64, 128], P('hd', 'hb', 'wb')
- grad_key: bfloat16 [12, 4, 4, 64, 128], P('hd', 'hb', 'wb')
- grad_value: bfloat16 [12, 4, 4, 64, 128], P('hd', 'hb', 'wb')
Inputs may be any that keep to these rules, and one draw needn't show every extreme that they name: sel_count[r, c] is the number of live entries of that query tile's list, from 1 to 8; entries of sel_tiles at positions sel_count or beyond are ignored, and entries may repeat.
All inputs are finite; a program needn't handle non-finite values.
Results may differ from a plain program's by a relative error of at most 0.022.
Values may be sent and summed in bfloat16 or wider, within the bound.
A program may use at most 64 MiB of HBM per device.

v0:
```python
import jax
import jax.numpy as jnp
from jax import lax
from jax.sharding import PartitionSpec as P


def with_halo(x, sides, width):
    for axis, dim in sides:
        size, length = (lax.axis_size(axis), x.shape[dim])
        up = [(i, (i + 1) % size) for i in range(size - 1)]
        down = [(j, i) for i, j in up]
        last = lax.slice_in_dim(x, length - width, length, axis=dim)
        first = lax.slice_in_dim(x, 0, width, axis=dim)
        before = lax.ppermute(last, axis, up)
        after = lax.ppermute(first, axis, down)
        x = jnp.concatenate([before, x, after], axis=dim)
    return x


def settle(values):
    return lax.optimization_barrier(values.astype(jnp.bfloat16)).astype(jnp.float32)


def tile_masks(tile_radius, sel_tiles, sel_count):
    band_rows, band_cols, picks = sel_tiles.shape
    tile_total = band_rows * band_cols
    tile_index = jnp.arange(tile_total, dtype=jnp.int32)
    row_of = tile_index // band_cols
    col_of = tile_index % band_cols
    spread = jnp.abs(row_of[:, None] - row_of[None, :]) + jnp.abs(col_of[:, None] - col_of[None, :])
    nearby = spread[None] <= tile_radius[:, None, None]
    live_pick = jnp.arange(picks, dtype=jnp.int32)[None, :] < sel_count.reshape(tile_total, 1)
    matches = (sel_tiles.reshape(tile_total, picks, 1) == tile_index[None, None, :]) & live_pick[
        :, :, None
    ]
    return nearby | jnp.any(matches, axis=1)[None]


def side_scores(queries, keyside, is_open, factor):
    scores = (
        jnp.einsum("hrid,hrjd->hrij", queries, keyside, preferred_element_type=jnp.float32) * factor
    )
    return jnp.where(is_open[:, None, None, None], scores, -jnp.inf)


def side_grad(probs, cotan, valside, delta, factor):
    slopes = jnp.einsum("hrid,hrjd->hrij", cotan, valside, preferred_element_type=jnp.float32)
    return (probs * (slopes - delta[..., None]) * factor).astype(jnp.bfloat16)


def edge_terms(queries, cotan, log_sum, delta, keyside, valside, is_open, factor):
    scores = (
        jnp.einsum("hrid,hrjd->hrij", queries, keyside, preferred_element_type=jnp.float32) * factor
    )
    probs = jnp.where(is_open[:, None, None, None], jnp.exp(scores - log_sum[..., None]), 0.0)
    slopes = jnp.einsum("hrid,hrjd->hrij", cotan, valside, preferred_element_type=jnp.float32)
    score_grad = (probs * (slopes - delta[..., None]) * factor).astype(jnp.bfloat16)
    key_term = jnp.einsum(
        "hrij,hrid->hrjd", score_grad, queries, preferred_element_type=jnp.float32
    )
    value_term = jnp.einsum(
        "hrij,hrid->hrjd", probs.astype(jnp.bfloat16), cotan, preferred_element_type=jnp.float32
    )
    return (key_term, value_term)


def on_device(query_rows, key_rows, value_rows, grad_out, sel_tiles, sel_count, tile_radius):
    head_count, tile_rows, tile_cols, tile_len, head_dim = query_rows.shape
    dev_tiles = tile_rows * tile_cols
    dev_rows = dev_tiles * tile_len
    factor = head_dim ** (-0.5)
    grid_shape = (head_count, tile_rows, tile_cols, tile_len)
    hb_index = lax.axis_index("hb")
    wb_index = lax.axis_index("wb")
    wb_count = lax.axis_size("wb")
    fringe = with_halo(jnp.stack((key_rows, value_rows, query_rows, grad_out)), (("wb", 3),), 1)
    band_keys, band_values, band_queries, band_cotan = (
        lax.all_gather(key_rows, "hb", axis=1, tiled=True),
        lax.all_gather(value_rows, "hb", axis=1, tiled=True),
        lax.all_gather(query_rows, "hb", axis=1, tiled=True),
        lax.all_gather(grad_out, "hb", axis=1, tiled=True),
    )
    band_tiles = band_keys.shape[1] * tile_cols
    allowed_all = tile_masks(tile_radius, sel_tiles, sel_count)
    own_start = hb_index * dev_tiles
    allowed_own = lax.dynamic_slice_in_dim(allowed_all, own_start, dev_tiles, 1)
    own_query = query_rows.reshape(head_count, dev_rows, head_dim)
    own_cotan = grad_out.reshape(head_count, dev_rows, head_dim)
    key_flat = band_keys.reshape(head_count, -1, head_dim)
    value_flat = band_values.reshape(head_count, -1, head_dim)
    shaped = (head_count, dev_tiles, tile_len, band_tiles, tile_len)
    scores = (
        jnp.einsum("hqd,hkd->hqk", own_query, key_flat, preferred_element_type=jnp.float32) * factor
    )
    scores = jnp.where(allowed_own[:, :, None, :, None], scores.reshape(shaped), -jnp.inf).reshape(
        head_count, dev_rows, -1
    )
    reach = tile_radius >= 1
    left_open = reach & (wb_index >= 1)
    right_open = reach & (wb_index < wb_count - 1)
    left_keys = fringe[0][:, :, 0]
    right_keys = fringe[0][:, :, -1]
    left_vals = fringe[1][:, :, 0]
    right_vals = fringe[1][:, :, -1]
    left_scores = side_scores(query_rows[:, :, 0], left_keys, left_open, factor)
    right_scores = side_scores(query_rows[:, :, -1], right_keys, right_open, factor)
    top = jnp.max(scores, axis=-1).reshape(grid_shape)
    top = top.at[:, :, 0].max(jnp.max(left_scores, axis=-1))
    top = top.at[:, :, -1].max(jnp.max(right_scores, axis=-1))
    total = jnp.sum(jnp.exp(scores - top.reshape(head_count, dev_rows, 1)), axis=-1).reshape(
        grid_shape
    )
    total = total.at[:, :, 0].add(jnp.sum(jnp.exp(left_scores - top[:, :, 0, :, None]), axis=-1))
    total = total.at[:, :, -1].add(jnp.sum(jnp.exp(right_scores - top[:, :, -1, :, None]), axis=-1))
    log_sum = top + jnp.log(total)
    probs = jnp.exp(scores - log_sum.reshape(head_count, dev_rows, 1))
    left_probs = jnp.exp(left_scores - log_sum[:, :, 0, :, None])
    right_probs = jnp.exp(right_scores - log_sum[:, :, -1, :, None])
    prob_half = probs.astype(jnp.bfloat16)
    output = jnp.einsum(
        "hqk,hkd->hqd", prob_half, value_flat, preferred_element_type=jnp.float32
    ).reshape(grid_shape + (head_dim,))
    output = output.at[:, :, 0].add(
        jnp.einsum(
            "hrij,hrjd->hrid",
            left_probs.astype(jnp.bfloat16),
            left_vals,
            preferred_element_type=jnp.float32,
        )
    )
    output = output.at[:, :, -1].add(
        jnp.einsum(
            "hrij,hrjd->hrid",
            right_probs.astype(jnp.bfloat16),
            right_vals,
            preferred_element_type=jnp.float32,
        )
    )
    delta = jnp.sum(grad_out.astype(jnp.float32) * output, axis=-1)
    edge_stats = with_halo(jnp.stack((log_sum, delta)), (("wb", 3),), 1)
    slopes = jnp.einsum("hqd,hkd->hqk", own_cotan, value_flat, preferred_element_type=jnp.float32)
    score_grad = (probs * (slopes - delta.reshape(head_count, dev_rows, 1)) * factor).astype(
        jnp.bfloat16
    )
    left_grad = side_grad(left_probs, grad_out[:, :, 0], left_vals, delta[:, :, 0], factor)
    right_grad = side_grad(right_probs, grad_out[:, :, -1], right_vals, delta[:, :, -1], factor)
    grad_query = jnp.einsum(
        "hqk,hkd->hqd", score_grad, key_flat, preferred_element_type=jnp.float32
    ).reshape(grid_shape + (head_dim,))
    grad_query = grad_query.at[:, :, 0].add(
        jnp.einsum("hrij,hrjd->hrid", left_grad, left_keys, preferred_element_type=jnp.float32)
    )
    grad_query = grad_query.at[:, :, -1].add(
        jnp.einsum("hrij,hrjd->hrid", right_grad, right_keys, preferred_element_type=jnp.float32)
    )
    band_stats = lax.all_gather(jnp.stack((log_sum, delta)), "hb", axis=2, tiled=True)
    all_query = band_queries.reshape(head_count, -1, head_dim)
    all_cotan = band_cotan.reshape(head_count, -1, head_dim)
    allowed_cols = lax.dynamic_slice_in_dim(allowed_all, own_start, dev_tiles, 2)
    reverse = (
        jnp.einsum(
            "hqd,hkd->hqk",
            all_query,
            key_rows.reshape(head_count, dev_rows, head_dim),
            preferred_element_type=jnp.float32,
        )
        * factor
    )
    rev_shape = (head_count, band_tiles, tile_len, dev_tiles, tile_len)
    row_sums = band_stats[0].reshape(head_count, band_tiles, tile_len, 1, 1)
    rev_probs = jnp.where(
        allowed_cols[:, :, None, :, None], jnp.exp(reverse.reshape(rev_shape) - row_sums), 0.0
    ).reshape(head_count, -1, dev_rows)
    rev_slopes = jnp.einsum(
        "hqd,hkd->hqk",
        all_cotan,
        value_rows.reshape(head_count, dev_rows, head_dim),
        preferred_element_type=jnp.float32,
    )
    rev_grad = (
        rev_probs * (rev_slopes - band_stats[1].reshape(head_count, -1, 1)) * factor
    ).astype(jnp.bfloat16)
    groups = lax.axis_size("hb")
    key_parts = jnp.einsum(
        "hgqk,hgqd->hgkd",
        rev_grad.reshape(head_count, groups, dev_rows, dev_rows),
        all_query.reshape(head_count, groups, dev_rows, head_dim),
        preferred_element_type=jnp.float32,
    )
    value_parts = jnp.einsum(
        "hgqk,hgqd->hgkd",
        rev_probs.astype(jnp.bfloat16).reshape(head_count, groups, dev_rows, dev_rows),
        all_cotan.reshape(head_count, groups, dev_rows, head_dim),
        preferred_element_type=jnp.float32,
    )
    key_band = jnp.sum(settle(key_parts), axis=1)
    value_band = jnp.sum(settle(value_parts), axis=1)
    key_grid = key_band.reshape(grid_shape + (head_dim,))
    value_grid = value_band.reshape(grid_shape + (head_dim,))
    left_key, left_value = edge_terms(
        fringe[2][:, :, 0],
        fringe[3][:, :, 0],
        edge_stats[0][:, :, 0],
        edge_stats[1][:, :, 0],
        key_rows[:, :, 0],
        value_rows[:, :, 0],
        left_open,
        factor,
    )
    right_key, right_value = edge_terms(
        fringe[2][:, :, -1],
        fringe[3][:, :, -1],
        edge_stats[0][:, :, -1],
        edge_stats[1][:, :, -1],
        key_rows[:, :, -1],
        value_rows[:, :, -1],
        right_open,
        factor,
    )
    key_grid = key_grid.at[:, :, 0].add(left_key).at[:, :, -1].add(right_key)
    value_grid = value_grid.at[:, :, 0].add(left_value).at[:, :, -1].add(right_value)
    return (
        grad_query.astype(jnp.bfloat16),
        key_grid.astype(jnp.bfloat16),
        value_grid.astype(jnp.bfloat16),
    )


def solution(mesh):
    return jax.shard_map(
        on_device,
        mesh=mesh,
        in_specs=(
            P("hd", "hb", "wb", None, None),
            P("hd", "hb", "wb", None, None),
            P("hd", "hb", "wb", None, None),
            P("hd", "hb", "wb", None, None),
            P(None, "wb", None),
            P(None, "wb"),
            P("hd"),
        ),
        out_specs=(
            P("hd", "hb", "wb", None, None),
            P("hd", "hb", "wb", None, None),
            P("hd", "hb", "wb", None, None),
        ),
        check_vma=False,
    )
```

profile of v0, /device:TPU:0, one launch (start us, length us, event | category | flops | bytes accessed | tf_op | source)
XLA Modules:
  0.0 72.3 jit_solution(1648671841766254662)
XLA Ops:
  0.6 0.9 %copy.247 = bf16[3,1,2,64,128]{4,3,0,2,1:T(8,128)(2,1)S(1)} copy(bf16[3,1,2,64,128]{4,3,2,1,0:T(8,128)(2,1)} %param.31) | data formatting | bytes 196608 | tf_op args[0]
  1.6 0.9 %copy-done.3 = bf16[3,1,2,64,128]{4,3,2,1,0:T(8,128)(2,1)S(1)} copy-done((bf16[3,1,2,64,128]{4,3,2,1,0:T(8,128)(2,1)S(1)}, bf16[3,1,2,64,128]{4,3,2,1,0:T(8,128)(2,1)}, u32[]{:S(2)}) %copy-start.3) | copy-done | bytes 98328
  2.5 0.9 %copy-done.1 = bf16[3,1,2,64,128]{4,3,2,1,0:T(8,128)(2,1)S(1)} copy-done((bf16[3,1,2,64,128]{4,3,2,1,0:T(8,128)(2,1)S(1)}, bf16[3,1,2,64,128]{4,3,2,1,0:T(8,128)(2,1)}, u32[]{:S(2)}) %copy-start.1) | copy-done | bytes 98328
  3.4 0.8 %fusion.86 = (bf16[4,3,1,1,64,128]{5,4,1,3,2,0:T(8,128)(2,1)}, bf16[4,3,1,1,64,128]{5,4,1,3,2,0:T(8,128)(2,1)}) fusion(bf16[4,3,1,2,64,128]{5,4,1,3,2,0:T(8,128)(2,1)S(1)} %pad_maximum_fusion.1), kind=kLoop, calls=%fused_computation.179 | loop fusion | bytes 786432 | tf_op jit(solution)/shard_map/slice | solution.py:12
  4.2 1.3 %collective-permute-start.1 = (bf16[4,3,1,1,64,128]{5,4,1,3,2,0:T(8,128)(2,1)}, bf16[4,3,1,1,64,128]{5,4,1,3,2,0:T(8,128)(2,1)}, u32[]{:S(2)}, u32[]{:S(2)}) collective-permute-start(bf16[4,3,1,1,64,128]{5,4,1,3,2,0:T(8,128)(2,1)} %get-tuple-element.167), channel_id=1, source_target_pairs={{4,0},{5,1},{6,2},{7,3},{12,8},{13,9},{14,10},{15,11},{20,16},{21,... | collective-permute-start | bytes 589832 | tf_op jit(solution)/shard_map/ppermute | solution.py:15
  5.5 6.2 %collective-permute-start = (bf16[4,3,1,1,64,128]{5,4,1,3,2,0:T(8,128)(2,1)}, bf16[4,3,1,1,64,128]{5,4,1,3,2,0:T(8,128)(2,1)}, u32[]{:S(2)}, u32[]{:S(2)}) collective-permute-start(bf16[4,3,1,1,64,128]{5,4,1,3,2,0:T(8,128)(2,1)} %get-tuple-element.166), channel_id=1, source_target_pairs={{0,4},{1,5},{2,6},{3,7},{8,12},{9,13},{10,14},{11,15},{16,20},{17,... | collective-permute-start | bytes 589832 | tf_op jit(solution)/shard_map/ppermute | solution.py:14
  11.7 7.6 %all_gather.15 = bf16[3,4,2,64,128]{4,3,2,1,0:T(8,128)(2,1)S(1)} all-gather(bf16[3,1,2,64,128]{4,3,2,1,0:T(8,128)(2,1)S(1)} %copy-done.1), channel_id=1, replica_groups=mesh['hb'=4,'wb'=2,'hd'=4] {'hb'}, dimensions={1}, use_global_device_ids=true | all-gather | bytes 491520 | tf_op jit(solution)/shard_map/all_gather | solution.py:78
  19.3 6.7 %all_gather.16 = bf16[3,4,2,64,128]{4,3,2,1,0:T(8,128)(2,1)S(1)} all-gather(bf16[3,1,2,64,128]{4,3,2,1,0:T(8,128)(2,1)S(1)} %copy-done.3), channel_id=1, replica_groups=mesh['hb'=4,'wb'=2,'hd'=4] {'hb'}, dimensions={1}, use_global_device_ids=true | all-gather | bytes 491520 | tf_op jit(solution)/shard_map/all_gather | solution.py:79
  26.0 0.7 copy-done.12
  27.6 0.7 copy-done.11
  28.4 6.6 %all_gather.17 = bf16[3,4,2,64,128]{4,3,2,1,0:T(8,128)(2,1)S(1)} all-gather(bf16[3,1,2,64,128]{4,3,2,1,0:T(8,128)(2,1)S(1)} %copy-done.2), channel_id=1, replica_groups=mesh['hb'=4,'wb'=2,'hd'=4] {'hb'}, dimensions={1}, use_global_device_ids=true | all-gather | bytes 491520 | tf_op jit(solution)/shard_map/all_gather | solution.py:80
  35.0 6.6 %all_gather.19 = bf16[3,4,2,64,128]{4,3,2,1,0:T(8,128)(2,1)S(1)} all-gather(bf16[3,1,2,64,128]{4,3,2,1,0:T(8,128)(2,1)S(1)} %copy-done), channel_id=1, replica_groups=mesh['hb'=4,'wb'=2,'hd'=4] {'hb'}, dimensions={1}, use_global_device_ids=true | all-gather | bytes 491520 | tf_op jit(solution)/shard_map/all_gather | solution.py:81
  41.9 0.7 %broadcast_in_dim.73 = pred[3,128,512]{2,1,0:T(32,128)(4,1)S(1)} reshape(pred[3,2,64,8,64]{4,3,2,1,0:T(8,128)(4,1)S(1)} %broadcast_in_dim.72) | data formatting | bytes 393216 | tf_op jit(solution)/shard_map/jit(_where)/broadcast_in_dim | solution.py:95
  43.2 1.4 %broadcast_in_dim.79 = pred[3,512,128]{1,2,0:T(32,128)(4,1)} reshape(pred[3,8,64,2,64]{2,1,4,3,0:T(8,128)(4,1)S(1)} %broadcast_in_dim.78) | data formatting | bytes 393216 | tf_op jit(solution)/shard_map/jit(_where)/broadcast_in_dim | solution.py:171
  44.7 1.1 %copy.206 = pred[3,512,128]{2,1,0:T(32,128)(4,1)S(1)} copy(pred[3,512,128]{1,2,0:T(32,128)(4,1)} %broadcast_in_dim.79) | data formatting | bytes 393216 | tf_op jit(solution)/shard_map/jit(_where)/broadcast_in_dim | solution.py:171
  45.8 1.1 %pad_maximum_fusion = bf16[4,3,1,4,64,128]{5,4,1,3,2,0:T(8,128)(2,1)S(1)} fusion(bf16[4,3,1,1,64,128]{5,4,1,3,2,0:T(8,128)(2,1)} %collective-permute-done.1, bf16[1,3,1,2,64,128]{5,4,1,3,2,0:T(8,128)(2,1)S(1)} %bitcast.253, bf16[1,3,1,2,64,128]{5,4,1,3,2,0:T(8,128)(2,1)S(1)} %bitcast.260, bf16[1,3,1,2,64,128]{5,4,1,3,2,0:T(8,128)(2,1)S(1)} %bitcast.251, ...), kind=kLoop, calls=%fused_computation.73 | loop fusion | flops 1966080 | bytes 1572864 | tf_op jit(solution)/shard_map/concatenate | solution.py:16
  47.0 0.8 %slice_bitcast_fusion = (bf16[3,1,4,64,128]{4,3,0,2,1:T(8,128)(2,1)}, bf16[3,1,4,64,128]{4,3,0,2,1:T(8,128)(2,1)}, bf16[3,1,4,64,128]{4,3,0,2,1:T(8,128)(2,1)}, bf16[3,1,4,64,128]{4,3,0,2,1:T(8,128)(2,1)S(1)}) fusion(bf16[4,3,1,4,64,128]{5,4,1,3,2,0:T(8,128)(2,1)S(1)} %pad_maximum_fusion), kind=kLoop, calls=%fused_computation.85 | loop fusion | bytes 1572864 | tf_op jit(solution)/shard_map/squeeze | solution.py:202
  49.7 0.9 %copy-done.5 = bf16[3,1,4,64,128]{4,3,0,2,1:T(8,128)(2,1)S(1)} copy-done((bf16[3,1,4,64,128]{4,3,0,2,1:T(8,128)(2,1)S(1)}, bf16[3,1,4,64,128]{4,3,0,2,1:T(8,128)(2,1)}, u32[]{:S(2)}) %copy-start.5) | copy-done | bytes 196632
  51.3 1.1 %fusion.10 = f32[3,128,128]{2,1,0:T(8,128)} fusion(bf16[3,512,128]{2,1,0:T(8,128)(2,1)S(1)} %bitcast.242, bf16[3,128,128]{2,1,0:T(8,128)(2,1)S(1)} %bitcast.249, bf16[3,512,128]{2,1,0:T(8,128)(2,1)S(1)} %bitcast.244, f32[3,128,512]{2,1,0:T(8,128)S(1)} %get-tuple-element.197, f32[3,128]{1,0:T(4,128)S(1)} %sub.230, f32[3,128]{1,0:T(4,128)S(1)} %sub.221), kind=kOutput, calls=%fused_computation.16 | convolution fusion | flops 101646336 | bytes 1870848 | tf_op jit(solution)/shard_map/hqk,hkd->hqd/dot_general | solution.py:147
  52.5 0.9 %copy.201 = f32[3,1,2,64,128]{4,3,0,2,1:T(8,128)S(1)} copy(f32[3,1,2,64,128]{4,3,2,0,1:T(8,128)} %bitcast.263) | data formatting | bytes 393216 | tf_op jit(solution)/shard_map/reshape | solution.py:149
  53.4 5.2 %all_gather.18 = f32[2,3,4,2,64]{4,1,3,2,0:T(4,128)S(1)} all-gather(f32[2,3,1,2,64]{4,1,3,2,0:T(4,128)S(1)} %pad_maximum_fusion.3), channel_id=1, replica_groups=mesh['hb'=4,'wb'=2,'hd'=4] {'hb'}, dimensions={2}, use_global_device_ids=true | all-gather | bytes 15360 | tf_op jit(solution)/shard_map/all_gather | solution.py:156
  59.9 1.3 %collective-permute-start.3 = (f32[2,3,1,1,64]{4,1,3,2,0:T(4,128)S(1)}, f32[2,3,1,1,64]{4,1,3,2,0:T(4,128)S(1)}, u32[]{:S(2)}, u32[]{:S(2)}) collective-permute-start(f32[2,3,1,1,64]{4,1,3,2,0:T(4,128)S(1)} %get-tuple-element.185), channel_id=1, source_target_pairs={{4,0},{5,1},{6,2},{7,3},{12,8},{13,9},{14,10},{15,11},{20,16},{21,... | collective-permute-start | bytes 4616 | tf_op jit(solution)/shard_map/ppermute | solution.py:15
  61.2 4.5 %collective-permute-start.2 = (f32[2,3,1,1,64]{4,1,3,2,0:T(4,128)S(1)}, f32[2,3,1,1,64]{4,1,3,2,0:T(4,128)S(1)}, u32[]{:S(2)}, u32[]{:S(2)}) collective-permute-start(f32[2,3,1,1,64]{4,1,3,2,0:T(4,128)S(1)} %get-tuple-element.184), channel_id=1, source_target_pairs={{0,4},{1,5},{2,6},{3,7},{8,12},{9,13},{10,14},{11,15},{16,20},{17,... | collective-permute-start | bytes 4616 | tf_op jit(solution)/shard_map/ppermute | solution.py:14
  68.3 0.8 %copy-done.7 = bf16[3,1,4,64,128]{4,3,0,2,1:T(8,128)(2,1)S(1)} copy-done((bf16[3,1,4,64,128]{4,3,0,2,1:T(8,128)(2,1)S(1)}, bf16[3,1,4,64,128]{4,3,0,2,1:T(8,128)(2,1)}, u32[]{:S(2)}) %copy-start.7) | copy-done | bytes 196632
  (104 shorter events, 11.4 us)
Async XLA Ops:
  0.6 0.9 %copy-start = (bf16[3,1,2,64,128]{4,3,2,1,0:T(8,128)(2,1)S(1)}, bf16[3,1,2,64,128]{4,3,2,1,0:T(8,128)(2,1)}, u32[]{:S(2)}) copy-start(bf16[3,1,2,64,128]{4,3,2,1,0:T(8,128)(2,1)} %param.34) | copy-start | bytes 294916
  1.6 0.9 %copy-start.3 = (bf16[3,1,2,64,128]{4,3,2,1,0:T(8,128)(2,1)S(1)}, bf16[3,1,2,64,128]{4,3,2,1,0:T(8,128)(2,1)}, u32[]{:S(2)}) copy-start(bf16[3,1,2,64,128]{4,3,2,1,0:T(8,128)(2,1)} %param.33) | copy-start | bytes 294916
  2.5 0.9 %copy-start.1 = (bf16[3,1,2,64,128]{4,3,2,1,0:T(8,128)(2,1)S(1)}, bf16[3,1,2,64,128]{4,3,2,1,0:T(8,128)(2,1)}, u32[]{:S(2)}) copy-start(bf16[3,1,2,64,128]{4,3,2,1,0:T(8,128)(2,1)} %param.32) | copy-start | bytes 294916
  4.2 41.6 %collective-permute-start.1 = (bf16[4,3,1,1,64,128]{5,4,1,3,2,0:T(8,128)(2,1)}, bf16[4,3,1,1,64,128]{5,4,1,3,2,0:T(8,128)(2,1)}, u32[]{:S(2)}, u32[]{:S(2)}) collective-permute-start(bf16[4,3,1,1,64,128]{5,4,1,3,2,0:T(8,128)(2,1)} %get-tuple-element.167), channel_id=1, source_target_pairs={{4,0},{5,1},{6,2},{7,3},{12,8},{13,9},{14,10},{15,11},{20,16},{21,... | collective-permute-start | bytes 589832 | tf_op jit(solution)/shard_map/ppermute | solution.py:15
  5.5 40.3 %collective-permute-start = (bf16[4,3,1,1,64,128]{5,4,1,3,2,0:T(8,128)(2,1)}, bf16[4,3,1,1,64,128]{5,4,1,3,2,0:T(8,128)(2,1)}, u32[]{:S(2)}, u32[]{:S(2)}) collective-permute-start(bf16[4,3,1,1,64,128]{5,4,1,3,2,0:T(8,128)(2,1)} %get-tuple-element.166), channel_id=1, source_target_pairs={{0,4},{1,5},{2,6},{3,7},{8,12},{9,13},{10,14},{11,15},{16,20},{17,... | collective-permute-start | bytes 589832 | tf_op jit(solution)/shard_map/ppermute | solution.py:14
  19.3 9.2 %copy-start.2 = (bf16[3,1,2,64,128]{4,3,2,1,0:T(8,128)(2,1)S(1)}, bf16[3,1,2,64,128]{4,3,2,1,0:T(8,128)(2,1)}, u32[]{:S(2)}) copy-start(bf16[3,1,2,64,128]{4,3,2,1,0:T(8,128)(2,1)} %param.31) | copy-start | bytes 294916
  26.0 0.7 copy-start.12
  26.7 0.7 copy-start.10
  27.6 0.7 copy-start.11
  47.8 0.7 copy-start.8
  49.7 0.9 %copy-start.5 = (bf16[3,1,4,64,128]{4,3,0,2,1:T(8,128)(2,1)S(1)}, bf16[3,1,4,64,128]{4,3,0,2,1:T(8,128)(2,1)}, u32[]{:S(2)}) copy-start(bf16[3,1,4,64,128]{4,3,0,2,1:T(8,128)(2,1)} %get-tuple-element.164) | copy-start | bytes 589828
  59.9 8.3 %collective-permute-start.3 = (f32[2,3,1,1,64]{4,1,3,2,0:T(4,128)S(1)}, f32[2,3,1,1,64]{4,1,3,2,0:T(4,128)S(1)}, u32[]{:S(2)}, u32[]{:S(2)}) collective-permute-start(f32[2,3,1,1,64]{4,1,3,2,0:T(4,128)S(1)} %get-tuple-element.185), channel_id=1, source_target_pairs={{4,0},{5,1},{6,2},{7,3},{12,8},{13,9},{14,10},{15,11},{20,16},{21,... | collective-permute-start | bytes 4616 | tf_op jit(solution)/shard_map/ppermute | solution.py:15
  61.2 7.0 %collective-permute-start.2 = (f32[2,3,1,1,64]{4,1,3,2,0:T(4,128)S(1)}, f32[2,3,1,1,64]{4,1,3,2,0:T(4,128)S(1)}, u32[]{:S(2)}, u32[]{:S(2)}) collective-permute-start(f32[2,3,1,1,64]{4,1,3,2,0:T(4,128)S(1)} %get-tuple-element.184), channel_id=1, source_target_pairs={{0,4},{1,5},{2,6},{3,7},{8,12},{9,13},{10,14},{11,15},{16,20},{17,... | collective-permute-start | bytes 4616 | tf_op jit(solution)/shard_map/ppermute | solution.py:14
  65.7 0.9 %copy-start.6 = (bf16[3,1,4,64,128]{4,3,0,2,1:T(8,128)(2,1)S(1)}, bf16[3,1,4,64,128]{4,3,0,2,1:T(8,128)(2,1)}, u32[]{:S(2)}) copy-start(bf16[3,1,4,64,128]{4,3,0,2,1:T(8,128)(2,1)} %get-tuple-element.164) | copy-start | bytes 589828
  65.8 1.0 %copy-start.9 = (bf16[3,1,4,64,128]{4,3,0,2,1:T(8,128)(2,1)S(1)}, bf16[3,1,4,64,128]{4,3,0,2,1:T(8,128)(2,1)}, u32[]{:S(2)}) copy-start(bf16[3,1,4,64,128]{4,3,0,2,1:T(8,128)(2,1)} %copy-done.8) | copy-start | bytes 589828
  68.2 0.9 %copy-start.7 = (bf16[3,1,4,64,128]{4,3,0,2,1:T(8,128)(2,1)S(1)}, bf16[3,1,4,64,128]{4,3,0,2,1:T(8,128)(2,1)}, u32[]{:S(2)}) copy-start(bf16[3,1,4,64,128]{4,3,0,2,1:T(8,128)(2,1)} %get-tuple-element.163) | copy-start | bytes 589828
  69.1 0.9 %copy-start.4 = (bf16[3,1,4,64,128]{4,3,0,2,1:T(8,128)(2,1)S(1)}, bf16[3,1,4,64,128]{4,3,0,2,1:T(8,128)(2,1)}, u32[]{:S(2)}) copy-start(bf16[3,1,4,64,128]{4,3,0,2,1:T(8,128)(2,1)} %get-tuple-element.162) | copy-start | bytes 589828
where the time goes:
time: 72.9 us; the launch traced here: 72.3 us
  blocking collectives  32.6 us (45%)
  local copies, waits for them, and re-layouts  17 us (23%)
  starting transfers between devices  13.3 us (18%)
  matrix products  5.82 us (8%)
  other arithmetic  2.38 us (3%)
  between operations  1.11 us (2%)
    ppermute x2, starting transfers between devices, with_halo(): before = lax.ppermute(last, axis, up)  10.8 us
    unnamed x34, local copies, waits for them, and re-layouts  9.75 us
    all_gather x1, blocking collectives, on_device(): lax.all_gather(key_rows, 'hb', axis=1, tiled=True)  7.56 us
    all_gather x1, blocking collectives, on_device(): lax.all_gather(value_rows, 'hb', axis=1, tiled=True)  6.69 us
    all_gather x1, blocking collectives, on_device(): lax.all_gather(query_rows, 'hb', axis=1, tiled=True)  6.58 us
    all_gather x1, blocking collectives, on_device(): lax.all_gather(grad_out, 'hb', axis=1, tiled=True)  6.56 us
    all_gather x1, blocking collectives, on_device(): lax.all_gather(jnp.stack((log_sum, delta)), 'hb', axis=2, tiled=True)  5.19 us
    broadcast_in_dim x3, local copies, waits for them, and re-layouts, on_device(): jnp.where(allowed_cols[:, :, None, :, None], jnp.exp(reverse.reshape(rev_...  2.72 us
  transfers between devices with their start and end apart: 4, of which 0 were waited for; matrix products, arithmetic and copies ran while one was open for 9% of the time, Pallas kernels for 0%

commit v1 on v0

v1 whole, which is shorter than its diff:
```python
import functools

import jax
import jax.numpy as jnp
from jax import lax
from jax.experimental import pallas as pl
from jax.experimental.pallas import tpu as pltpu
from jax.sharding import PartitionSpec as P

MESH = pl.DeviceIdType.MESH
F32 = jnp.float32
BF16 = jnp.bfloat16
NT = (((1,), (1,)), ((), ()))
NN = (((1,), (0,)), ((), ()))
TN = (((0,), (0,)), ((), ()))


def dot(a, b, dims):
    return lax.dot_general(a, b, dims, preferred_element_type=F32)


def kernel(
    dims,
    q_hbm, k_hbm, v_hbm, g_hbm, sel_ref, count_ref, radius_ref,
    dq_ref, dk_ref, dv_ref,
    qg, kv, acc_own, acc_chip, tx_sib, rx_sib, tx_chip, rx_chip, tx_edge, rx_edge,
    q_sem, kv_sem, s_kvsib, r_kvsib, s_kvchip, r_kvchip, s_relay, r_relay, s_kvedge, r_kvedge,
    s_psib, r_psib, s_pchip, r_pchip, s_pedge, r_pedge,
):
    heads, trows, tcols, tile, picks, n_hb, n_wb, factor = dims
    rows = trows * tcols * tile
    chips = n_hb // 2
    me = lax.axis_index("hb")
    w = lax.axis_index("wb")
    chip, core = me // 2, me % 2
    sib = chip * 2 + 1 - core
    to_chip = {j: ((chip + j) % chips) * 2 + core for j in range(1, chips)}
    from_chip = {j: ((chip + chips - j) % chips) * 2 + core for j in range(1, chips)}
    if n_wb == 1:
        links = []
    elif n_wb == 2:
        links = [(None, 1 - w, 0, 0, (1 - w) * (tcols - 1))]
    else:
        links = [(w > 0, w - 1, 0, 1, 0), (w < n_wb - 1, w + 1, 1, 0, tcols - 1)]

    def guarded(there, fn):
        if there is None:
            fn()
        else:
            pl.when(there)(fn)

    def remote(src, dst, send, recv, axis, to):
        return pltpu.make_async_remote_copy(
            src_ref=src, dst_ref=dst, send_sem=send, recv_sem=recv,
            device_id={axis: to}, device_id_type=MESH,
        )

    own_kv = []
    for h in range(heads):
        own_kv.append((
            pltpu.make_async_copy(k_hbm.at[h], kv.at[0, h, pl.ds(0, rows)], kv_sem.at[h, 0]),
            pltpu.make_async_copy(v_hbm.at[h], kv.at[1, h, pl.ds(0, rows)], kv_sem.at[h, 1]),
        ))
        for c in own_kv[-1]:
            c.start()
    own_q = [
        pltpu.make_async_copy(q_hbm, qg.at[0], q_sem.at[0]),
        pltpu.make_async_copy(g_hbm, qg.at[1], q_sem.at[1]),
    ]
    for c in own_q:
        c.start()

    barrier = pltpu.get_barrier_semaphore()
    pl.semaphore_signal(barrier, inc=1, device_id={"hb": sib}, device_id_type=MESH)
    for j in range(1, chips):
        pl.semaphore_signal(barrier, inc=1, device_id={"hb": to_chip[j]}, device_id_type=MESH)
    for there, peer, _, _, _ in links:
        def hello(peer=peer):
            pl.semaphore_signal(barrier, inc=1, device_id={"wb": peer}, device_id_type=MESH)
        guarded(there, hello)
    if n_wb > 2:
        for slot, (there, _, _, _, _) in enumerate(links):
            def blank(slot=slot):
                at = n_hb * rows + slot * trows * tile
                kv[:, :, pl.ds(at, trows * tile), :] = jnp.zeros(
                    (2, heads, trows * tile, kv.shape[-1]), BF16)
            pl.when(jnp.logical_not(there))(blank)
    greeted = chips
    for there, _, _, _, _ in links:
        greeted = greeted + (1 if there is None else jnp.where(there, 1, 0))
    pl.semaphore_wait(barrier, greeted)

    def slot_at(s):
        return pl.ds(s * rows, rows)

    def edge_at(slot, r):
        return pl.ds(n_hb * rows + (slot * trows + r) * tile, tile)

    def kv_chip(h, j):
        return remote(kv.at[:, h, slot_at(0)], kv.at[:, h, slot_at(2 * j)],
                      s_kvchip.at[h, j], r_kvchip.at[h, j], "hb", to_chip[j])

    def kv_sib(h):
        return remote(kv.at[:, h, slot_at(0)], kv.at[:, h, slot_at(1)],
                      s_kvsib.at[h], r_kvsib.at[h], "hb", sib)

    def relay(h, j):
        return remote(kv.at[:, h, slot_at(2 * j)], kv.at[:, h, slot_at(2 * j + 1)],
                      s_relay.at[h, j], r_relay.at[h, j], "hb", sib)

    def own_tile(r, col):
        return pl.ds(pl.multiple_of((r * tcols + col) * tile, tile), tile)

    def kv_edge(h, link, r, arriving=False):
        _, peer, here, away, col = link
        slot = here if arriving else away
        return remote(kv.at[:, h, own_tile(r, col)], kv.at[:, h, edge_at(slot, r)],
                      s_kvedge.at[h, away, r], r_kvedge.at[h, slot, r], "wb", peer)

    def p_sib(h, j):
        return remote(tx_sib.at[h, j], rx_sib.at[h, j], s_psib.at[h, j], r_psib.at[h, j], "hb", sib)

    def p_chip(h, j):
        return remote(tx_chip.at[h, j], rx_chip.at[h, j],
                      s_pchip.at[h, j], r_pchip.at[h, j], "hb", from_chip[j])

    def p_edge(h, link, arriving=False):
        _, peer, here, away, _ = link
        slot = here if arriving else away
        return remote(tx_edge.at[h, here], rx_edge.at[h, slot],
                      s_pedge.at[h, here], r_pedge.at[h, slot], "wb", peer)

    for h in range(heads):
        for c in own_kv[h]:
            c.wait()
        for j in range(1, chips):
            kv_chip(h, j).start()
        kv_sib(h).start()
        for link in links:
            def send(link=link, h=h):
                for r in range(trows):
                    kv_edge(h, link, r).start()
            guarded(link[0], send)

    lane_tile = lax.broadcasted_iota(jnp.int32, (1, rows), 1) // tile
    lane_row = me * trows + lane_tile // tcols
    lane_col = lane_tile % tcols
    chosen = []
    for s in range(picks):
        entry = jnp.full((1, rows), -1, jnp.int32)
        for r in range(trows):
            for c in range(tcols):
                row = me * trows + r
                value = jnp.where(s < count_ref[row, c], sel_ref[row, c, s], -1)
                entry = jnp.where(lane_tile == r * tcols + c, value, entry)
        chosen.append(entry)
    spread, picked = [], []
    for s in range(n_hb):
        j = s // 2
        group = ((chip + chips - j) % chips) * 2 + (core if s % 2 == 0 else 1 - core)
        for r in range(trows):
            for c in range(tcols):
                key_row = group * trows + r
                spread.append(jnp.abs(lane_row - key_row) + jnp.abs(lane_col - c))
                at = key_row * tcols + c
                hit = functools.reduce(jnp.logical_or, [e == at for e in chosen])
                picked.append(hit)
    beside = []
    for there, _, slot, _, col in links:
        for r in range(trows):
            near = lane_tile == r * tcols + col
            if there is not None:
                near = jnp.logical_and(near, there)
            beside.append(near)

    for c in own_q:
        c.wait()

    def compute(h):
        q = qg[0, h]
        g = qg[1, h]
        keys = kv[0, h]
        vals = kv[1, h]
        radius = radius_ref[h]
        bias = [jnp.where(jnp.logical_or(sp <= radius, pk), 0.0, -jnp.inf)
                for sp, pk in zip(spread, picked)]
        bias += [jnp.where(jnp.logical_and(near, radius >= 1), 0.0, -jnp.inf) for near in beside]
        scores = dot(keys, q, NT)
        slopes = dot(vals, g, NT)
        s_t = [scores[i * tile:(i + 1) * tile] * factor + b for i, b in enumerate(bias)]
        d_t = [slopes[i * tile:(i + 1) * tile] for i in range(len(bias))]
        top = jnp.max(functools.reduce(jnp.maximum, s_t), axis=0, keepdims=True)
        e_t = [jnp.exp(s - top) for s in s_t]
        total = jnp.sum(functools.reduce(jnp.add, e_t), axis=0, keepdims=True)
        mixed = jnp.sum(functools.reduce(jnp.add, [e * d for e, d in zip(e_t, d_t)]),
                        axis=0, keepdims=True)
        inverse = 1.0 / total
        delta = mixed * inverse
        probs = [e * inverse for e in e_t]
        half = jnp.concatenate([p.astype(BF16) for p in probs], axis=0)
        grad = jnp.concatenate(
            [(p * ((d - delta) * factor)).astype(BF16) for p, d in zip(probs, d_t)], axis=0)
        return q, g, keys, half, grad

    for h in range(heads):
        for j in range(1, chips):
            kv_chip(h, j).wait_recv()
            relay(h, j).start()
        kv_sib(h).wait_recv()
        for link in links:
            def arrive(link=link, h=h):
                for r in range(trows):
                    kv_edge(h, link, r, True).wait_recv()
            guarded(link[0], arrive)
        for j in range(1, chips):
            relay(h, j).wait_recv()
        q, g, keys, half, grad = compute(h)
        if chips > 1:
            far = slice(2 * rows, n_hb * rows)
            far_parts = (dot(grad[far], q, NN), dot(half[far], g, NN))
            for j in range(1, chips):
                at = (2 * j - 2) * rows
                for i, part in enumerate(far_parts):
                    tx_sib[h, j, i] = part[at + rows:at + 2 * rows].astype(BF16)
                    acc_chip[h, j, i] = part[at:at + rows]
                p_sib(h, j).start()
        near_parts = (dot(grad[:2 * rows], q, NN), dot(half[:2 * rows], g, NN))
        for i, part in enumerate(near_parts):
            tx_sib[h, 0, i] = part[rows:].astype(BF16)
            acc_own[h, i] = part[:rows]
        p_sib(h, 0).start()
        if links:
            edge_parts = (dot(grad[n_hb * rows:], q, NN), dot(half[n_hb * rows:], g, NN))
            for link in links:
                here = link[2]
                for i, part in enumerate(edge_parts):
                    tx_edge[h, here, i] = part[here * trows * tile:(here + 1) * trows * tile].astype(BF16)
                guarded(link[0], lambda link=link, h=h: p_edge(h, link).start())
        dq_ref[h] = dot(grad, keys, TN).astype(BF16)
        for j in range(1, chips):
            p_sib(h, j).wait_recv()
            for i in range(2):
                tx_chip[h, j, i] = (acc_chip[h, j, i] + rx_sib[h, j, i].astype(F32)).astype(BF16)
            p_chip(h, j).start()

    for h in range(heads):
        p_sib(h, 0).wait_recv()
        for link in links:
            there, _, here, _, col = link

            def add_edge(link=link, here=here, col=col, h=h):
                p_edge(h, link, True).wait_recv()
                for i in range(2):
                    for r in range(trows):
                        at = own_tile(r, col)
                        acc_own[h, i, at] += rx_edge[h, here, i, pl.ds(r * tile, tile)].astype(F32)
            guarded(there, add_edge)
        totals = [acc_own[h, i] + rx_sib[h, 0, i].astype(F32) for i in range(2)]
        for j in range(1, chips):
            p_chip(h, j).wait_recv()
            for i in range(2):
                totals[i] = totals[i] + rx_chip[h, j, i].astype(F32)
        dk_ref[h] = totals[0].astype(BF16)
        dv_ref[h] = totals[1].astype(BF16)

    for h in range(heads):
        kv_sib(h).wait_send()
        p_sib(h, 0).wait_send()
        for j in range(1, chips):
            kv_chip(h, j).wait_send()
            relay(h, j).wait_send()
            p_sib(h, j).wait_send()
            p_chip(h, j).wait_send()
        for link in links:
            def drain(link=link, h=h):
                for r in range(trows):
                    kv_edge(h, link, r).wait_send()
                p_edge(h, link).wait_send()
            guarded(link[0], drain)


def on_device(n_hb, n_wb, query_rows, key_rows, value_rows, grad_out, sel_tiles, sel_count, tile_radius):
    heads, trows, tcols, tile, depth = query_rows.shape
    picks = sel_tiles.shape[-1]
    rows = trows * tcols * tile
    chips = n_hb // 2
    sides = max(1, min(2, n_wb - 1))
    used = min(2, n_wb - 1)
    flat = (heads, rows, depth)
    keys = n_hb * rows + used * trows * tile
    dma = pltpu.SemaphoreType.DMA
    dims = (heads, trows, tcols, tile, picks, n_hb, n_wb, depth ** -0.5)
    any_spec = pl.BlockSpec(memory_space=pl.ANY)
    smem = pl.BlockSpec(memory_space=pltpu.SMEM)
    vmem = pl.BlockSpec(memory_space=pltpu.VMEM)
    out = jax.ShapeDtypeStruct(flat, BF16)
    results = pl.pallas_call(
        functools.partial(kernel, dims),
        out_shape=(out, out, out),
        in_specs=[any_spec] * 4 + [smem] * 3,
        out_specs=(vmem,) * 3,
        scratch_shapes=[
            pltpu.VMEM((2,) + flat, BF16),
            pltpu.VMEM((2, heads, keys, depth), BF16),
            pltpu.VMEM((heads, 2, rows, depth), F32),
            pltpu.VMEM((heads, chips, 2, rows, depth), F32),
            pltpu.VMEM((heads, chips, 2, rows, depth), BF16),
            pltpu.VMEM((heads, chips, 2, rows, depth), BF16),
            pltpu.VMEM((heads, chips, 2, rows, depth), BF16),
            pltpu.VMEM((heads, chips, 2, rows, depth), BF16),
            pltpu.VMEM((heads, sides, 2, trows * tile, depth), BF16),
            pltpu.VMEM((heads, sides, 2, trows * tile, depth), BF16),
            dma((2,)), dma((heads, 2)),
            dma((heads,)), dma((heads,)),
            dma((heads, chips)), dma((heads, chips)),
            dma((heads, chips)), dma((heads, chips)),
            dma((heads, sides, trows)), dma((heads, sides, trows)),
            dma((heads, chips)), dma((heads, chips)),
            dma((heads, chips)), dma((heads, chips)),
            dma((heads, sides)), dma((heads, sides)),
        ],
        compiler_params=pltpu.CompilerParams(
            collective_id=0, has_side_effects=True, vmem_limit_bytes=48 * 1024 * 1024),
        cost_estimate=pl.CostEstimate(
            flops=10 * heads * rows * keys * depth,
            bytes_accessed=14 * heads * rows * depth,
            transcendentals=heads * rows * keys),
    )(
        query_rows.reshape(flat), key_rows.reshape(flat), value_rows.reshape(flat),
        grad_out.reshape(flat), sel_tiles, sel_count, tile_radius,
    )
    return tuple(r.reshape(query_rows.shape) for r in results)


def solution(mesh):
    block = P("hd", "hb", "wb", None, None)
    return jax.shard_map(
        functools.partial(on_device, mesh.shape["hb"], mesh.shape["wb"]),
        mesh=mesh,
        in_specs=(block, block, block, block, P(None, "wb", None), P(None, "wb"), P("hd")),
        out_specs=(block, block, block),
        check_vma=False,
    )
```

time: 72.9 us -> 27.5 us (0.38)
  blocking collectives: 32.6 us -> 0 us
  Pallas kernels: 0 us -> 19.7 us
  starting transfers between devices: 13.3 us -> 0 us
  local copies, waits for them, and re-layouts: 17 us -> 6.83 us
  matrix products: 5.82 us -> 0 us
  other arithmetic: 2.38 us -> 0 us
    all_gather x5 -> x0, blocking collectives: 32.6 us -> none  [the longest x1 7.56 us: on_device(): lax.all_gather(key_rows, 'hb', axis=1, tiled=True)]
    pallas_call x0 -> x1, Pallas kernels: none -> 19.7 us  [on_device(): pl.pallas_call(functools.partial(kernel, dims), out_shape=(out, out, out)...]
    ppermute x4 -> x0, starting transfers between devices: 13.3 us -> none  [the longest x2 10.8 us: with_halo(): before = lax.ppermute(last, axis, up)]
    dot_general x19 -> x0, matrix products: 5.82 us -> none  [the longest x1 1.13 us: on_device(): jnp.einsum('hqk,hkd->hqd', score_grad, key_flat, preferred_element_type=j...]
    broadcast_in_dim x5 -> x0, local copies, waits for them, and re-layouts: 3.63 us -> none  [the longest x3 2.72 us: on_device(): jnp.where(allowed_cols[:, :, None, :, None], jnp.exp(reverse.reshape(rev_...]
    unnamed x34 -> x18, local copies, waits for them, and re-layouts: 9.75 us -> 6.83 us
    reshape x8 -> x0, local copies, waits for them, and re-layouts: 1.16 us -> none  [the longest x1 0.94 us: on_device(): grad_query = jnp.einsum('hqk,hkd->hqd', score_grad, key_flat, preferred_e...]
    concatenate x2 -> x0, other arithmetic: 1.15 us -> none  [with_halo(): x = jnp.concatenate([before, x, after], axis=dim)]
  transfers between devices with their start and end apart: 4 -> 0, of which waited for: 0 -> 0; matrix products, arithmetic and copies ran while one was open for 9% -> 0% of each run, Pallas kernels for 0% -> 0%
where the time goes in v1:
time: 27.5 us; the launch traced here: 27.2 us
  Pallas kernels  19.7 us (72%)
  local copies, waits for them, and re-layouts  6.83 us (25%)
  between operations  0.66 us (2%)
    pallas_call x1, Pallas kernels, on_device(): pl.pallas_call(functools.partial(kernel, dims), out_shape=(out, out, out)...  19.7 us
    unnamed x18, local copies, waits for them, and re-layouts  6.83 us

profile of v1, /device:TPU:0, one launch (start us, length us, event | category | flops | bytes accessed | tf_op | source)
XLA Modules:
  0.0 27.2 jit_solution(7265919088549370774)
XLA Ops:
  0.6 0.0 copy-start.4
  0.6 0.0 copy-start.6
  0.7 0.7 %copy-done.6 = s32[4,2]{0,1:T(2,128)S(1)} copy-done((s32[4,2]{0,1:T(2,128)S(1)}, s32[4,2]{0,1:T(2,128)}, u32[]{:S(2)}) %copy-start.6) | copy-done | bytes 56
  1.3 0.0 copy-start.5
  1.3 0.1 copy.10.count_ref
  1.4 0.0 copy-done.4
  1.4 0.6 %copy-done.5 = s32[3]{0:T(128)S(1)} copy-done((s32[3]{0:T(128)S(1)}, s32[3]{0:T(128)}, u32[]{:S(2)}) %copy-start.5) | copy-done | bytes 36
  2.0 0.0 copy-start
  2.0 0.9 %copy-done = bf16[3,1,2,64,128]{4,3,2,1,0:T(8,128)(2,1)S(1)} copy-done((bf16[3,1,2,64,128]{4,3,2,1,0:T(8,128)(2,1)S(1)}, bf16[3,1,2,64,128]{4,3,2,1,0:T(8,128)(2,1)}, u32[]{:S(2)}) %copy-start) | copy-done | bytes 98328
  2.9 0.0 copy-start.1
  2.9 0.9 %copy-done.1 = bf16[3,1,2,64,128]{4,3,2,1,0:T(8,128)(2,1)S(1)} copy-done((bf16[3,1,2,64,128]{4,3,2,1,0:T(8,128)(2,1)S(1)}, bf16[3,1,2,64,128]{4,3,2,1,0:T(8,128)(2,1)}, u32[]{:S(2)}) %copy-start.1) | copy-done | bytes 98328
  3.8 0.0 copy-start.2
  3.8 0.9 %copy-done.2 = bf16[3,1,2,64,128]{4,3,2,1,0:T(8,128)(2,1)S(1)} copy-done((bf16[3,1,2,64,128]{4,3,2,1,0:T(8,128)(2,1)S(1)}, bf16[3,1,2,64,128]{4,3,2,1,0:T(8,128)(2,1)}, u32[]{:S(2)}) %copy-start.2) | copy-done | bytes 98328
  4.7 0.0 copy-start.3
  4.7 0.9 %copy-done.3 = bf16[3,1,2,64,128]{4,3,2,1,0:T(8,128)(2,1)S(1)} copy-done((bf16[3,1,2,64,128]{4,3,2,1,0:T(8,128)(2,1)S(1)}, bf16[3,1,2,64,128]{4,3,2,1,0:T(8,128)(2,1)}, u32[]{:S(2)}) %copy-start.3) | copy-done | bytes 98328
  5.6 19.7 %shard_map.94 = (bf16[3,128,128]{2,1,0:T(8,128)(2,1)S(1)}, bf16[3,128,128]{2,1,0:T(8,128)(2,1)S(1)}, bf16[3,128,128]{2,1,0:T(8,128)(2,1)S(1)}) custom-call(bf16[3,128,128]{2,1,0:T(8,128)(2,1)S(1)} %bitcast.16, bf16[3,128,128]{2,1,0:T(8,128)(2,1)S(1)} %bitcast.17, bf16[3,128,128]{2,1,0:T(8,128)(2,1)S(1)} %bitcast.18, bf16[3,128,128]{2,1,0:T(8,128)(2,1)S(1)} %bitcast.19, ...), custom_call_target="tpu_custom_call" | custom-call | flops 283115520 | bytes 688128 | tf_op jit(solution)/shard_map/pallas_call | solution.py:297
  25.3 0.6 %copy.17 = bf16[3,1,2,64,128]{4,3,2,1,0:T(8,128)(2,1)} copy(bf16[3,1,2,64,128]{4,3,2,1,0:T(8,128)(2,1)S(1)} %bitcast.15) | data formatting | bytes 196608
  25.9 0.6 %copy.18 = bf16[3,1,2,64,128]{4,3,2,1,0:T(8,128)(2,1)} copy(bf16[3,1,2,64,128]{4,3,2,1,0:T(8,128)(2,1)S(1)} %bitcast.14) | data formatting | bytes 196608
  26.5 0.6 %copy.19 = bf16[3,1,2,64,128]{4,3,2,1,0:T(8,128)(2,1)} copy(bf16[3,1,2,64,128]{4,3,2,1,0:T(8,128)(2,1)S(1)} %bitcast.13) | data formatting | bytes 196608
Async XLA Ops:
  0.6 0.8 %copy-start.4 = (s32[4,2,8]{2,1,0:T(2,128)S(1)}, s32[4,2,8]{2,1,0:T(2,128)}, u32[]{:S(2)}) copy-start(s32[4,2,8]{2,1,0:T(2,128)} %sel_ref.1) | copy-start | bytes 772
  0.6 0.7 %copy-start.6 = (s32[4,2]{0,1:T(2,128)S(1)}, s32[4,2]{0,1:T(2,128)}, u32[]{:S(2)}) copy-start(s32[4,2]{0,1:T(2,128)} %param.12) | copy-start | bytes 100
  1.3 0.7 %copy-start.5 = (s32[3]{0:T(128)S(1)}, s32[3]{0:T(128)}, u32[]{:S(2)}) copy-start(s32[3]{0:T(128)} %radius_ref.1) | copy-start | bytes 40
  2.0 0.9 %copy-start = (bf16[3,1,2,64,128]{4,3,2,1,0:T(8,128)(2,1)S(1)}, bf16[3,1,2,64,128]{4,3,2,1,0:T(8,128)(2,1)}, u32[]{:S(2)}) copy-start(bf16[3,1,2,64,128]{4,3,2,1,0:T(8,128)(2,1)} %param.7) | copy-start | bytes 294916
  2.9 0.9 %copy-start.1 = (bf16[3,1,2,64,128]{4,3,2,1,0:T(8,128)(2,1)S(1)}, bf16[3,1,2,64,128]{4,3,2,1,0:T(8,128)(2,1)}, u32[]{:S(2)}) copy-start(bf16[3,1,2,64,128]{4,3,2,1,0:T(8,128)(2,1)} %param.8) | copy-start | bytes 294916
  3.8 0.9 %copy-start.2 = (bf16[3,1,2,64,128]{4,3,2,1,0:T(8,128)(2,1)S(1)}, bf16[3,1,2,64,128]{4,3,2,1,0:T(8,128)(2,1)}, u32[]{:S(2)}) copy-start(bf16[3,1,2,64,128]{4,3,2,1,0:T(8,128)(2,1)} %param.9) | copy-start | bytes 294916
  4.7 0.9 %copy-start.3 = (bf16[3,1,2,64,128]{4,3,2,1,0:T(8,128)(2,1)S(1)}, bf16[3,1,2,64,128]{4,3,2,1,0:T(8,128)(2,1)}, u32[]{:S(2)}) copy-start(bf16[3,1,2,64,128]{4,3,2,1,0:T(8,128)(2,1)} %param.10) | copy-start | bytes 294916
